TPU v7x, 256 devices: a whole 4x4x8 slice. The times are simulated.
256 devices in a mesh: grp: 4 (over x), grid: 64 (over y, z, core).
Axes of the slice: x: 4, y: 4, z: 8, core: 2. Of those that a mesh axis runs over, the one named last changes fastest.
Arguments:
- orbitals: float32 [512, 262144], P('grp', 'grid'), may hold values from -6 to 6
- anchors: int32 [512, 3], replicated, may hold values from 0 to 31
- pair_slots: int32 [256, 4, 2], replicated, may hold values from -1 to 511, as said below
Outputs:
- exchange_term: float32 [512, 262144], P('grp', 'grid')
Inputs may be any that keep to these rules, and one draw needn't show every extreme that they name: `pair_slots`: row k lists the pairs of owner k, the device with index k in the order grp, grid; its first slots hold pairs of two different orbital numbers and its other slots hold -1 in both columns. Exactly 512 slots hold pairs in all, no row holds more than 4, and some row holds exactly 4.
All inputs are finite; a program needn't handle non-finite values.
Results may differ from a plain program's by a relative error of at most 0.0003.
Values sent between devices are 32-bit elements; how exact they have to be, the bound alone decides.
No kernel may reach another device: no remote copies, remote signals or barrier semaphores. Data moves between devices by JAX's collectives and lax.ppermute only.
A program may use at most 128 MiB of HBM per device.

v0:
```python
import jax
import jax.numpy as jnp
from jax import lax
from jax.sharding import PartitionSpec as P

B = 64
PAIR_DEV = 2
ITERS = 3


def shift_field(field, offset, extent):
    plane_size = extent * extent
    padded_x = jnp.pad(field, ((extent, extent), (0, 0)))
    moved = lax.dynamic_slice_in_dim(padded_x, extent - offset[0], extent, 0)
    padded_yz = jnp.pad(moved, ((0, 0), (plane_size, plane_size)))
    linear = offset[1] * extent + offset[2]
    moved = lax.dynamic_slice_in_dim(padded_yz, plane_size - linear, plane_size, 1)
    cells = lax.broadcasted_iota(jnp.int32, (1, plane_size), 1)
    coord_y = cells // extent - offset[1]
    coord_z = cells % extent - offset[2]
    inside = (coord_y >= 0) & (coord_y < extent) & (coord_z >= 0) & (coord_z < extent)
    return jnp.where(inside, moved, jnp.zeros_like(moved))


def operate(field, extent):
    padded_x = jnp.pad(field, ((1, 1), (0, 0)))
    beside = padded_x[2:] + padded_x[:-2]
    padded_y = jnp.pad(field, ((0, 0), (extent, extent)))
    beside = beside + padded_y[:, 2 * extent :] + padded_y[:, : -2 * extent]
    padded_z = jnp.pad(field, ((0, 0), (1, 1)))
    cells = lax.broadcasted_iota(jnp.int32, (1, field.shape[1]), 1) % extent
    upper_z = jnp.where(cells < extent - 1, padded_z[:, 2:], jnp.zeros_like(field))
    lower_z = jnp.where(cells > 0, padded_z[:, :-2], jnp.zeros_like(field))
    return 6.0 * field - beside - upper_z - lower_z


def conjugate(density, extent):
    potential = jnp.zeros_like(density)
    resid = density
    direction = density
    norm_now = jnp.sum(resid * resid)
    for turn in range(ITERS):
        image = operate(direction, extent)
        step_len = norm_now / jnp.sum(direction * image)
        potential = potential + step_len * direction
        resid = resid - step_len * image
        norm_next = jnp.sum(resid * resid)
        direction = resid + norm_next / norm_now * direction
        norm_now = norm_next
    return potential


def pair_terms(field_a, field_b, offset, extent):
    partner = shift_field(field_b, offset, extent)
    density = field_a * partner
    potential = conjugate(density, extent)
    term_a = potential * partner
    term_b = shift_field(potential * field_a, -offset, extent)
    return (term_a, term_b)


def deal_evenly(pair_slots, owner_count, each_owner):
    flat_slots = pair_slots.reshape(-1, 2)
    filled = (flat_slots[:, 0] >= 0).astype(jnp.int32)
    order = jnp.arange(flat_slots.shape[0], dtype=jnp.int32)
    position = jnp.sum(jnp.where(order[None, :] < order[:, None], filled[None, :], 0), axis=1)
    wanted = lax.broadcasted_iota(jnp.int32, (owner_count, each_owner), 1) * owner_count
    wanted = (wanted + lax.broadcasted_iota(jnp.int32, (owner_count, each_owner), 0)).reshape(-1)
    matched = (position[None, :] == wanted[:, None]) & (filled[None, :] == 1)
    picked = jnp.dot(matched.astype(jnp.int32), flat_slots)
    return picked.reshape(owner_count, each_owner, 2)


def body(orbitals, anchors, pair_slots):
    extent = B
    grid_count = lax.axis_size("grid")
    owner_count = lax.axis_size("grp") * grid_count
    group_idx = lax.axis_index("grp")
    place_idx = lax.axis_index("grid")
    assignment = deal_evenly(pair_slots, owner_count, PAIR_DEV)
    filled = assignment[..., 0] >= 0
    safe_ids = jnp.maximum(assignment, 0)
    pieces = lax.all_gather(orbitals, "grp", axis=0, tiled=True)
    group_table = lax.dynamic_slice_in_dim(safe_ids, group_idx * grid_count, grid_count, 0)
    gather_ids = jnp.transpose(group_table, (1, 2, 0))
    outgoing = pieces[gather_ids]
    arrived = lax.all_to_all(outgoing, "grid", split_axis=2, concat_axis=2, tiled=True)
    owner_idx = group_idx * grid_count + place_idx
    own_pairs = safe_ids[owner_idx]
    own_filled = filled[owner_idx]
    offsets = anchors[own_pairs[:, 1]] - anchors[own_pairs[:, 0]]

    def solve_slot(slot_item):
        boxes_pair, offset, flag = slot_item
        term_a, term_b = pair_terms(boxes_pair[0], boxes_pair[1], offset, extent)
        weight_flag = jnp.where(flag, 1.0, 0.0).astype(jnp.float32)
        return jnp.stack([term_a, term_b]) * weight_flag

    terms = lax.map(solve_slot, (arrived, offsets, own_filled))
    returned = lax.all_to_all(terms, "grid", split_axis=2, concat_axis=2, tiled=True)
    flat_terms = returned.reshape(-1, returned.shape[-1])
    summed = jax.ops.segment_sum(flat_terms, gather_ids.reshape(-1), num_segments=anchors.shape[0])
    return lax.psum_scatter(summed, "grp", scatter_dimension=0, tiled=True)


def solution(mesh):
    return jax.shard_map(
        body,
        mesh=mesh,
        in_specs=(P("grp", "grid"), P(), P()),
        out_specs=P("grp", "grid"),
        check_vma=False,
    )
```

profile of v0, /device:TPU:1, one launch (start us, length us, event | category | flops | bytes accessed | tf_op | source)
XLA Modules:
  0.0 504.9 jit_solution(9031635187783980270)
XLA Ops:
  8.8 1.4 broadcast_maximum_fusion
  10.3 88.3 %all-gather.2.cloned.1.call-done = f32[512,4096]{1,0:T(8,128)} async-done(((f32[128,4096]{1,0:T(8,128)}), f32[512,4096]{1,0:T(8,128)}) %all-gather.2.cloned.1.call-update) | async-done | bytes 8388624 | tf_op jit(solution)/shard_map/all_gather | solution.py:83
  98.7 9.0 %gather_fusion = f32[256,4096]{1,0:T(8,128)} fusion(f32[512,4096]{1,0:T(8,128)} %all-gather.2.cloned.1.call-done, s32[1024]{0:T(1024)S(1)} %pad_clamp_fusion.2), kind=kCustom, calls=%fused_computation | custom fusion | bytes 8389632 | tf_op jit(solution)/shard_map/gather | solution.py:86
  107.7 7.4 %copy.23 = f32[2,2,64,4096]{3,1,0,2:T(2,128)} copy(f32[2,2,64,4096]{3,2,1,0:T(8,128)} %bitcast.60) | data formatting | bytes 8388608 | tf_op jit(solution)/shard_map/gather | solution.py:86
  115.0 11.0 %all-to-all-start = ((f32[2,2,64,4096]{3,1,0,2:T(2,128)}), f32[2,2,64,4096]{3,1,0,2:T(2,128)}, u32[]{:S(2)}, u32[]{:S(2)}) async-start(f32[2,2,64,4096]{3,1,0,2:T(2,128)} %copy.23), calls=%async_computation | async-start | bytes 8388608 | tf_op jit(solution)/shard_map/all_to_all | solution.py:87
  128.0 93.9 %all-to-all-done = f32[2,2,64,4096]{3,1,0,2:T(2,128)} async-done(((f32[2,2,64,4096]{3,1,0,2:T(2,128)}), f32[2,2,64,4096]{3,1,0,2:T(2,128)}, u32[]{:S(2)}, u32[]{:S(2)}) %all-to-all-start) | async-done | bytes 4194336 | tf_op jit(solution)/shard_map/all_to_all | solution.py:87
  222.0 77.1 %while.13 = (s32[]{:T(128)}, f32[2,2,64,4096]{3,1,0,2:T(2,128)}, f32[2,2,64,4096]{3,1,0,2:T(2,128)}, s32[2,3]{1,0:T(2,128)S(1)}, pred[2]{0:T(512)(128)(4,1)S(1)}...) while((s32[]{:T(128)}, f32[2,2,64,4096]{3,1,0,2:T(2,128)}, ...), condition=%wide.region_8.9_spmd, body=%wide.region_1.8_spmd.sunk | while | flops 22224920 | bytes 64017664 | solution.py:99
  225.2 4.4 constant_dynamic-slice_fusion.5
  230.3 1.3 fusion.76
  231.6 1.0 fusion.77
  232.6 1.8 multiply_reduce_fusion.9
  238.1 1.8 multiply_reduce_fusion.11
  243.6 1.8 fusion.79
  246.7 3.9 multiply_bitcast_fusion.2
  252.0 1.3 pad_dynamic-slice_fusion.7
  254.5 1.2 fusion.80
  257.5 3.0 copy_dynamic-update-slice_fusion.2
  263.7 4.4 constant_dynamic-slice_fusion.5
  268.9 1.3 fusion.76
  270.1 1.0 fusion.77
  271.1 1.8 multiply_reduce_fusion.9
  276.6 1.8 multiply_reduce_fusion.11
  282.2 1.8 fusion.79
  285.3 3.9 multiply_bitcast_fusion.2
  290.5 1.3 pad_dynamic-slice_fusion.7
  293.1 1.2 fusion.80
  296.1 3.0 copy_dynamic-update-slice_fusion.2
  299.1 6.0 %all-to-all-start.1 = ((f32[2,2,64,4096]{3,1,0,2:T(2,128)}), f32[2,2,64,4096]{3,1,0,2:T(2,128)}, u32[]{:S(2)}, u32[]{:S(2)}) async-start(f32[2,2,64,4096]{3,1,0,2:T(2,128)} %get-tuple-element.107), calls=%async_computation.1 | async-start | bytes 8388608 | tf_op jit(solution)/shard_map/all_to_all | solution.py:100
  305.2 95.8 %all-to-all-done.1 = f32[2,2,64,4096]{3,1,0,2:T(2,128)} async-done(((f32[2,2,64,4096]{3,1,0,2:T(2,128)}), f32[2,2,64,4096]{3,1,0,2:T(2,128)}, u32[]{:S(2)}, u32[]{:S(2)}) %all-to-all-start.1) | async-done | bytes 4194336 | tf_op jit(solution)/shard_map/all_to_all | solution.py:100
  401.0 6.6 %copy.28 = f32[2,2,64,4096]{3,2,1,0:T(8,128)} copy(f32[2,2,64,4096]{3,1,0,2:T(2,128)} %all-to-all-done.1) | data formatting | bytes 8388608 | tf_op jit(solution)/shard_map/all_to_all | solution.py:100
  407.5 11.3 %scatter_custom_fusion = f32[512,4096]{1,0:T(8,128)} fusion(s32[256]{0:T(256)S(1)} %reshape.253, f32[256,4096]{1,0:T(8,128)} %bitcast.61, f32[]{:T(128)} %constant.159.clone.1), kind=kCustom, calls=%fused_computation.90 | custom fusion | flops 1048576 | bytes 8389120 | tf_op jit(solution)/shard_map/scatter-add | solution.py:102
  418.8 79.2 %reduce-scatter.2.cloned.1.call-done = f32[128,4096]{1,0:T(8,128)} async-done(((f32[512,4096]{1,0:T(8,128)}), f32[128,4096]{1,0:T(8,128)}) %reduce-scatter.2.cloned.1.call-update) | async-done | bytes 2097168 | tf_op jit(solution)/shard_map/reduce_scatter | solution.py:103
  (64 shorter events, 14.0 us)
Async XLA Ops:
  6.5 92.1 %all-gather.2.cloned.1.call-start = ((), (), s32[]{:S(2)}) async-start(), calls=%async_computation.3 | async-start | bytes 10485760 | tf_op jit(solution)/shard_map/all_gather | solution.py:83
  115.0 11.0 %copy-start.3 = (s32[512,3]{0,1:T(4,128)S(1)}, s32[512,3]{0,1:T(4,128)}, u32[]{:S(2)}) copy-start(s32[512,3]{0,1:T(4,128)} %param.6) | copy-start | bytes 18436
  115.0 106.9 %all-to-all-start = ((f32[2,2,64,4096]{3,1,0,2:T(2,128)}), f32[2,2,64,4096]{3,1,0,2:T(2,128)}, u32[]{:S(2)}, u32[]{:S(2)}) async-start(f32[2,2,64,4096]{3,1,0,2:T(2,128)} %copy.23), calls=%async_computation | async-start | bytes 8388608 | tf_op jit(solution)/shard_map/all_to_all | solution.py:87
  229.6 4.8 copy-start
  230.3 2.3 copy-start.1
  250.7 6.7 %copy-start.2 = (f32[1,1,64,4096]{3,2,1,0:T(8,128)S(1)}, f32[1,1,64,4096]{3,2,1,0:T(8,128)}, u32[]{:S(2)}) copy-start(f32[1,1,64,4096]{3,2,1,0:T(8,128)} %get-tuple-element.231) | copy-start | bytes 3145732 | tf_op jit(solution)/shard_map/while
  268.1 4.8 copy-start
  268.9 2.3 copy-start.1
  289.2 6.7 %copy-start.2 = (f32[1,1,64,4096]{3,2,1,0:T(8,128)S(1)}, f32[1,1,64,4096]{3,2,1,0:T(8,128)}, u32[]{:S(2)}) copy-start(f32[1,1,64,4096]{3,2,1,0:T(8,128)} %get-tuple-element.231) | copy-start | bytes 3145732 | tf_op jit(solution)/shard_map/while
  299.1 101.9 %all-to-all-start.1 = ((f32[2,2,64,4096]{3,1,0,2:T(2,128)}), f32[2,2,64,4096]{3,1,0,2:T(2,128)}, u32[]{:S(2)}, u32[]{:S(2)}) async-start(f32[2,2,64,4096]{3,1,0,2:T(2,128)} %get-tuple-element.107), calls=%async_computation.1 | async-start | bytes 8388608 | tf_op jit(solution)/shard_map/all_to_all | solution.py:100
  305.1 193.0 %reduce-scatter.2.cloned.1.call-start = ((), (), s32[]{:S(2)}) async-start(), calls=%async_computation.4 | async-start | bytes 10485760 | tf_op jit(solution)/shard_map/reduce_scatter | solution.py:103
Sparse Core Ops, SparseCore 0:
  9.2 89.4 all-gather.1
  419.0 79.0 reduce-scatter.1
where the time goes:
time: 506 us; the launch traced here: 505 us
  waiting for transfers between devices  358 us (71%)
  local copies, waits for them, and re-layouts  47.1 us (9%)
  other arithmetic  43.2 us (9%)
  loops' own time  24.6 us (5%)
  starting transfers between devices  17.1 us (3%)
  between operations  13.5 us (3%)
    all_to_all x1, waiting for transfers between devices, body(): lax.all_to_all(terms, 'grid', split_axis=2, concat_axis=2, tiled=True)  95.8 us
    all_to_all x1, waiting for transfers between devices, body(): lax.all_to_all(outgoing, 'grid', split_axis=2, concat_axis=2, tiled=True)  93.9 us
    all_gather x1, waiting for transfers between devices, body(): pieces = lax.all_gather(orbitals, 'grp', axis=0, tiled=True)  88.3 us
    reduce_scatter x1, waiting for transfers between devices, body(): return lax.psum_scatter(summed, 'grp', scatter_dimension=0, tiled=True)  79.2 us
    another operation x1, loops' own time, body(): terms = lax.map(solve_slot, (arrived, offsets, own_filled))  24.6 us
    gather x2, local copies, waits for them, and re-layouts, body(): outgoing = pieces[gather_ids]  16.4 us
    scatter-add x1, other arithmetic, body(): jax.ops.segment_sum(flat_terms, gather_ids.reshape(-1), num_segments=anch...  11.3 us
    all_to_all x1, starting transfers between devices, body(): lax.all_to_all(outgoing, 'grid', split_axis=2, concat_axis=2, tiled=True)  11 us
  transfers between devices with their start and end apart: 4, of which 4 were waited for; matrix products, arithmetic and copies ran while one was open for 1% of the time, Pallas kernels for 0%

commit v1 on v0

--- a/solution.py
+++ b/solution.py
@@ -6,6 +6,23 @@
 B = 64
 PAIR_DEV = 2
 ITERS = 3
+
+
+def extend_pairs_all(page, across):
+    dev_n = lax.axis_size(across)
+    vals = [(dev_j, (dev_j + 1) % dev_n) for dev_j in range(dev_n)]
+    frames = [(dev_j, (dev_j - 1) % dev_n) for dev_j in range(dev_n)]
+    a_next, local_part = ([page], [page])
+    for _ in range(dev_n // 2):
+        x_next = lax.ppermute(a_next[-1], across, vals)
+        a_next.append(x_next)
+    for _ in range((dev_n - 1) // 2):
+        aux = lax.ppermute(local_part[-1], across, frames)
+        local_part.append(aux)
+    arr_now = jnp.concatenate([*a_next[::-1], *local_part[1:]], axis=0)
+    taken_in = lax.axis_index(across)
+    long_array = jnp.roll(arr_now, shift=(taken_in - dev_n // 2) * page.shape[0], axis=0)
+    return long_array
 
 
 def shift_field(field, offset, extent):
@@ -80,7 +97,7 @@
     assignment = deal_evenly(pair_slots, owner_count, PAIR_DEV)
     filled = assignment[..., 0] >= 0
     safe_ids = jnp.maximum(assignment, 0)
-    pieces = lax.all_gather(orbitals, "grp", axis=0, tiled=True)
+    pieces = extend_pairs_all(orbitals, "grp")
     group_table = lax.dynamic_slice_in_dim(safe_ids, group_idx * grid_count, grid_count, 0)
     gather_ids = jnp.transpose(group_table, (1, 2, 0))
     outgoing = pieces[gather_ids]

time: 506 us -> 526 us (1.040)
  starting transfers between devices: 17.1 us -> 29.1 us
  local copies, waits for them, and re-layouts: 47.1 us -> 58.6 us
  waiting for transfers between devices: 358 us -> 352 us
    all_gather x1 -> x0, waiting for transfers between devices: 88.3 us -> none  [body(): pieces = lax.all_gather(orbitals, 'grp', axis=0, tiled=True)]
    ppermute x0 -> x3, waiting for transfers between devices: none -> 84 us  [the longest x2 84 us: extend_pairs_all(): x_next = lax.ppermute(a_next[-1], across, vals)]
    all_to_all x1, starting transfers between devices: 11 us -> 17.1 us  [body(): lax.all_to_all(outgoing, 'grid', split_axis=2, concat_axis=2, tiled=True)]
    ppermute x0 -> x3, starting transfers between devices: none -> 5.93 us  [the longest x2 3.93 us: extend_pairs_all(): x_next = lax.ppermute(a_next[-1], across, vals)]
    unnamed x4 -> x13, local copies, waits for them, and re-layouts: 0.98 us -> 6.9 us
  transfers between devices with their start and end apart: 4 -> 6, of which waited for: 4 -> 5; matrix products, arithmetic and copies ran while one was open for 1% -> 1% of each run, Pallas kernels for 0% -> 0%
where the time goes in v1:
time: 526 us; the launch traced here: 523 us
  waiting for transfers between devices  352 us (67%)
  local copies, waits for them, and re-layouts  58.6 us (11%)
  other arithmetic  43.2 us (8%)
  starting transfers between devices  29.1 us (6%)
  loops' own time  25 us (5%)
  between operations  13.8 us (3%)
    all_to_all x1, waiting for transfers between devices, body(): lax.all_to_all(terms, 'grid', split_axis=2, concat_axis=2, tiled=True)  95.8 us
    all_to_all x1, waiting for transfers between devices, body(): lax.all_to_all(outgoing, 'grid', split_axis=2, concat_axis=2, tiled=True)  93.9 us
    ppermute x2, waiting for transfers between devices, extend_pairs_all(): x_next = lax.ppermute(a_next[-1], across, vals)  84 us
    reduce_scatter x1, waiting for transfers between devices, body(): return lax.psum_scatter(summed, 'grp', scatter_dimension=0, tiled=True)  78.1 us
    another operation x1, loops' own time, body(): terms = lax.map(solve_slot, (arrived, offsets, own_filled))  25 us
    all_to_all x1, starting transfers between devices, body(): lax.all_to_all(outgoing, 'grid', split_axis=2, concat_axis=2, tiled=True)  17.1 us
    gather x2, local copies, waits for them, and re-layouts, body(): outgoing = pieces[gather_ids]  16.4 us
    scatter-add x1, other arithmetic, body(): jax.ops.segment_sum(flat_terms, gather_ids.reshape(-1), num_segments=anch...  11.3 us
  transfers between devices with their start and end apart: 6, of which 5 were waited for; matrix products, arithmetic and copies ran while one was open for 1% of the time, Pallas kernels for 0%

profile of v1, /device:TPU:1, one launch (start us, length us, event | category | flops | bytes accessed | tf_op | source)
XLA Modules:
  0.0 522.9 jit_solution(15622221826311450193)
XLA Ops:
  6.5 2.0 collective-permute-start
  8.6 44.5 %collective-permute-done = f32[128,4096]{1,0:T(8,128)S(1)} collective-permute-done((f32[128,4096]{1,0:T(8,128)}, f32[128,4096]{1,0:T(8,128)S(1)}, u32[]{:S(2)}, u32[]{:S(2)}) %collective-permute-start) | collective-permute-done | bytes 2097184 | tf_op jit(solution)/shard_map/ppermute | solution.py:17
  53.1 1.9 collective-permute-start.1
  55.0 2.0 collective-permute-start.2
  60.1 39.5 %collective-permute-done.1 = f32[128,4096]{1,0:T(8,128)} collective-permute-done((f32[128,4096]{1,0:T(8,128)S(1)}, f32[128,4096]{1,0:T(8,128)}, u32[]{:S(2)}, u32[]{:S(2)}) %collective-permute-start.1) | collective-permute-done | bytes 2097184 | tf_op jit(solution)/shard_map/ppermute | solution.py:17
  99.6 1.7 constant_dynamic-update-slice_fusion.7
  101.7 1.7 constant_dynamic-update-slice_fusion.4
  103.4 1.7 constant_dynamic-update-slice_fusion.3
  105.5 1.7 constant_dynamic-update-slice_fusion
  107.3 3.8 constant_dynamic-slice_fusion.3
  111.1 9.0 %gather_fusion = f32[256,4096]{1,0:T(8,128)} fusion(f32[512,4096]{1,0:T(8,128)} %constant_dynamic-slice_fusion.3, s32[1024]{0:T(1024)S(1)} %pad_clamp_fusion.2), kind=kCustom, calls=%fused_computation | custom fusion | bytes 8389632 | tf_op jit(solution)/shard_map/gather | solution.py:103
  120.1 7.4 %copy.23 = f32[2,2,64,4096]{3,1,0,2:T(2,128)} copy(f32[2,2,64,4096]{3,2,1,0:T(8,128)} %bitcast.60) | data formatting | bytes 8388608 | tf_op jit(solution)/shard_map/gather | solution.py:103
  127.5 17.1 %all-to-all-start = ((f32[2,2,64,4096]{3,1,0,2:T(2,128)}), f32[2,2,64,4096]{3,1,0,2:T(2,128)}, u32[]{:S(2)}, u32[]{:S(2)}) async-start(f32[2,2,64,4096]{3,1,0,2:T(2,128)} %copy.23), calls=%async_computation | async-start | bytes 8388608 | tf_op jit(solution)/shard_map/all_to_all | solution.py:104
  146.5 93.9 %all-to-all-done = f32[2,2,64,4096]{3,1,0,2:T(2,128)} async-done(((f32[2,2,64,4096]{3,1,0,2:T(2,128)}), f32[2,2,64,4096]{3,1,0,2:T(2,128)}, u32[]{:S(2)}, u32[]{:S(2)}) %all-to-all-start) | async-done | bytes 4194336 | tf_op jit(solution)/shard_map/all_to_all | solution.py:104
  240.5 77.5 %while.13 = (s32[]{:T(128)}, f32[2,2,64,4096]{3,1,0,2:T(2,128)}, f32[2,2,64,4096]{3,1,0,2:T(2,128)}, s32[2,3]{1,0:T(2,128)S(1)}, pred[2]{0:T(512)(128)(4,1)S(1)}...) while((s32[]{:T(128)}, f32[2,2,64,4096]{3,1,0,2:T(2,128)}, ...), condition=%wide.region_8.9_spmd, body=%wide.region_1.8_spmd.sunk | while | flops 22224920 | bytes 64017664 | solution.py:116
  243.8 4.4 constant_dynamic-slice_fusion.6
  251.3 1.8 multiply_reduce_fusion.9
  256.7 1.8 multiply_reduce_fusion.11
  262.3 1.8 fusion.79
  265.4 3.9 multiply_bitcast_fusion.2
  276.2 3.0 copy_dynamic-update-slice_fusion.2
  282.4 4.4 constant_dynamic-slice_fusion.6
  289.8 1.8 multiply_reduce_fusion.9
  295.3 1.8 multiply_reduce_fusion.11
  300.9 1.8 fusion.79
  303.9 3.9 multiply_bitcast_fusion.2
  314.8 3.0 copy_dynamic-update-slice_fusion.2
  317.9 6.0 %all-to-all-start.1 = ((f32[2,2,64,4096]{3,1,0,2:T(2,128)}), f32[2,2,64,4096]{3,1,0,2:T(2,128)}, u32[]{:S(2)}, u32[]{:S(2)}) async-start(f32[2,2,64,4096]{3,1,0,2:T(2,128)} %get-tuple-element.107), calls=%async_computation.1 | async-start | bytes 8388608 | tf_op jit(solution)/shard_map/all_to_all | solution.py:117
  324.1 95.8 %all-to-all-done.1 = f32[2,2,64,4096]{3,1,0,2:T(2,128)} async-done(((f32[2,2,64,4096]{3,1,0,2:T(2,128)}), f32[2,2,64,4096]{3,1,0,2:T(2,128)}, u32[]{:S(2)}, u32[]{:S(2)}) %all-to-all-start.1) | async-done | bytes 4194336 | tf_op jit(solution)/shard_map/all_to_all | solution.py:117
  419.9 6.6 %copy.28 = f32[2,2,64,4096]{3,2,1,0:T(8,128)} copy(f32[2,2,64,4096]{3,1,0,2:T(2,128)} %all-to-all-done.1) | data formatting | bytes 8388608 | tf_op jit(solution)/shard_map/all_to_all | solution.py:117
  426.4 11.3 %scatter_custom_fusion = f32[512,4096]{1,0:T(8,128)} fusion(s32[256]{0:T(256)S(1)} %reshape.253, f32[256,4096]{1,0:T(8,128)} %bitcast.61, f32[]{:T(128)} %constant.180.clone.1), kind=kCustom, calls=%fused_computation.90 | custom fusion | flops 1048576 | bytes 8389120 | tf_op jit(solution)/shard_map/scatter-add | solution.py:119
  437.7 78.1 %reduce-scatter.2.cloned.1.call-done = f32[128,4096]{1,0:T(8,128)} async-done(((f32[512,4096]{1,0:T(8,128)}), f32[128,4096]{1,0:T(8,128)}) %reduce-scatter.2.cloned.1.call-update) | async-done | bytes 2097168 | tf_op jit(solution)/shard_map/reduce_scatter | solution.py:120
  (78 shorter events, 24.9 us)
Async XLA Ops:
  6.5 46.6 %collective-permute-start = (f32[128,4096]{1,0:T(8,128)}, f32[128,4096]{1,0:T(8,128)S(1)}, u32[]{:S(2)}, u32[]{:S(2)}) collective-permute-start(f32[128,4096]{1,0:T(8,128)} %param.5), channel_id=1, source_target_pairs={{0,64},{64,128},{128,192},{192,0},{1,65},{65,129},{129,193},{193,1... | collective-permute-start | bytes 6291464 | tf_op jit(solution)/shard_map/ppermute | solution.py:17
  53.1 46.5 %collective-permute-start.1 = (f32[128,4096]{1,0:T(8,128)S(1)}, f32[128,4096]{1,0:T(8,128)}, u32[]{:S(2)}, u32[]{:S(2)}) collective-permute-start(f32[128,4096]{1,0:T(8,128)S(1)} %collective-permute-done), channel_id=1, source_target_pairs={{0,64},{64,128},{128,192},{192,0},{1,65},{65,129},{129,193},{193,1... | collective-permute-start | bytes 6291464 | tf_op jit(solution)/shard_map/ppermute | solution.py:17
  55.0 46.7 %collective-permute-start.2 = (f32[128,4096]{1,0:T(8,128)}, f32[128,4096]{1,0:T(8,128)}, u32[]{:S(2)}, u32[]{:S(2)}) collective-permute-start(f32[128,4096]{1,0:T(8,128)} %param.5), channel_id=1, source_target_pairs={{0,192},{64,0},{128,64},{192,128},{1,193},{65,1},{129,65},{193,129... | collective-permute-start | bytes 6291464 | tf_op jit(solution)/shard_map/ppermute | solution.py:20
  60.1 41.4 %copy-start.3 = (f32[128,4096]{1,0:T(8,128)S(1)}, f32[128,4096]{1,0:T(8,128)}, u32[]{:S(2)}) copy-start(f32[128,4096]{1,0:T(8,128)} %param.5) | copy-start | bytes 6291460
  127.5 17.1 %copy-start.4 = (s32[512,3]{0,1:T(4,128)S(1)}, s32[512,3]{0,1:T(4,128)}, u32[]{:S(2)}) copy-start(s32[512,3]{0,1:T(4,128)} %param.6) | copy-start | bytes 18436
  127.5 113.0 %all-to-all-start = ((f32[2,2,64,4096]{3,1,0,2:T(2,128)}), f32[2,2,64,4096]{3,1,0,2:T(2,128)}, u32[]{:S(2)}, u32[]{:S(2)}) async-start(f32[2,2,64,4096]{3,1,0,2:T(2,128)} %copy.23), calls=%async_computation | async-start | bytes 8388608 | tf_op jit(solution)/shard_map/all_to_all | solution.py:104
  248.2 4.8 copy-start
  249.0 2.3 copy-start.1
  269.3 6.7 %copy-start.2 = (f32[1,1,64,4096]{3,2,1,0:T(8,128)S(1)}, f32[1,1,64,4096]{3,2,1,0:T(8,128)}, u32[]{:S(2)}) copy-start(f32[1,1,64,4096]{3,2,1,0:T(8,128)} %get-tuple-element.231) | copy-start | bytes 3145732 | tf_op jit(solution)/shard_map/while
  286.8 4.8 copy-start
  287.6 2.3 copy-start.1
  307.8 6.7 %copy-start.2 = (f32[1,1,64,4096]{3,2,1,0:T(8,128)S(1)}, f32[1,1,64,4096]{3,2,1,0:T(8,128)}, u32[]{:S(2)}) copy-start(f32[1,1,64,4096]{3,2,1,0:T(8,128)} %get-tuple-element.231) | copy-start | bytes 3145732 | tf_op jit(solution)/shard_map/while
  317.9 101.9 %all-to-all-start.1 = ((f32[2,2,64,4096]{3,1,0,2:T(2,128)}), f32[2,2,64,4096]{3,1,0,2:T(2,128)}, u32[]{:S(2)}, u32[]{:S(2)}) async-start(f32[2,2,64,4096]{3,1,0,2:T(2,128)} %get-tuple-element.107), calls=%async_computation.1 | async-start | bytes 8388608 | tf_op jit(solution)/shard_map/all_to_all | solution.py:117
  324.0 191.8 %reduce-scatter.2.cloned.1.call-start = ((), (), s32[]{:S(2)}) async-start(), calls=%async_computation.3 | async-start | bytes 10485760 | tf_op jit(solution)/shard_map/reduce_scatter | solution.py:120
Sparse Core Ops, SparseCore 0:
  437.8 77.9 reduce-scatter.1
